TPU v7x, 128 devices: a whole 4x4x4 slice. The times are simulated.
128 devices in a mesh: grp: 4 (over x), gx: 4 (over z_lo, core), gy: 8 (over z_hi, y).
Axes of the slice: x: 4, y: 4, z: 4 (z_hi: 2, z_lo: 2; z = z_hi * 2 + z_lo), core: 2. Of those that a mesh axis runs over, the one named last changes fastest.
Arguments:
- flow_state: float32 [8, 768, 128, 128], P(None, ('grp', 'gx'), 'gy'), may hold values from -90 to 90
- speeds: float32 [3, 8], replicated, may hold values from 0.3 to 1.2
- viscosity: float32 [8], replicated, may hold values from 0.02 to 0.2
- reaction: float32 [8, 8], replicated, may hold values from -2 to 2
- start_basis: float32 [768, 96], replicated, may hold values from -6 to 6
- slab_table: int32 [8, 8, 1], replicated, may hold values from 0 to 15; in each aligned block of 8 rows (0 to 7, 8 to 15, ..., all dimensions but the last counted through in order) at most 2 rows name the same one
Outputs:
- final_state: float32 [8, 768, 128, 128], P(None, ('grp', 'gx'), 'gy')
- core_slots: float32 [256, 96, 8, 2, 128], P(('grp', 'gx', 'gy'))
Inputs may be any that keep to these rules, and one draw needn't show every extreme that they name: slab_table[t, u, 0] names the slab that stores unit u of row t; within each row t no slab is named by more than 2 units, a bound that some block reaches.
All inputs are finite; a program needn't handle non-finite values.
Results may differ from a plain program's by a relative error of at most 0.0034.
Values may be sent and summed in bfloat16 or wider, within the bound.
A program may use at most 256 MiB of HBM per device.

v0:
```python
import jax
import jax.numpy as jnp
from jax import lax
from jax.sharding import PartitionSpec as P

V = 8
NX = 768
R = 96
NZ = 128
YB = 2
NEWTON = 5


slope_weights = (0.8, -0.2, 4.0 / 105.0, -1.0 / 280.0)
curve_weights = (1.6, -0.2, 8.0 / 315.0, -1.0 / 560.0)
curve_center = -205.0 / 72.0
time_step = 0.2


def extended(shard, sides, width):
    for axis, dim in sides:
        peers, length = (lax.axis_size(axis), shard.shape[dim])
        up = [(i, (i + 1) % peers) for i in range(peers)]
        down = [(j, i) for i, j in up]
        last = lax.slice_in_dim(shard, length - width, length, axis=dim)
        initial = lax.slice_in_dim(shard, 0, width, axis=dim)
        before = lax.ppermute(last, axis, up)
        after = lax.ppermute(initial, axis, down)
        shard = jnp.concatenate([before, shard, after], axis=dim)
    return shard


def tendency(padded, speeds, viscosity, reaction):
    center = padded[:, 4:-4, 4:-4, :]
    width_first = center.shape[1]
    width_second = center.shape[2]
    diffusion = viscosity[:, None, None, None]
    speed_one = speeds[0][:, None, None, None]
    speed_two = speeds[1][:, None, None, None]
    speed_three = speeds[2][:, None, None, None]
    summed = 3.0 * curve_center * diffusion * center
    summed = summed + jnp.einsum("kj,jxyz->kxyz", reaction, center, precision=lax.Precision.HIGHEST)
    for offset in range(1, 5):
        slope_weight = slope_weights[offset - 1]
        curve_weight = curve_weights[offset - 1]
        spread = curve_weight * diffusion
        summed = summed + (
            (spread - slope_weight * speed_one)
            * padded[:, 4 + offset : 4 + offset + width_first, 4 : 4 + width_second, :]
            + (spread + slope_weight * speed_one)
            * padded[:, 4 - offset : 4 - offset + width_first, 4 : 4 + width_second, :]
            + (spread - slope_weight * speed_two)
            * padded[:, 4 : 4 + width_first, 4 + offset : 4 + offset + width_second, :]
            + (spread + slope_weight * speed_two)
            * padded[:, 4 : 4 + width_first, 4 - offset : 4 - offset + width_second, :]
            + (spread - slope_weight * speed_three) * jnp.roll(center, -offset, 3)
            + (spread + slope_weight * speed_three) * jnp.roll(center, offset, 3)
        )
    return summed


def extend(field):
    return extended(field, ((("grp", "gx"), 1), ("gy", 2)), 4)


def on_device(flow_state, speeds, viscosity, reaction, start_basis, slab_table):
    first = flow_state + time_step * tendency(extend(flow_state), speeds, viscosity, reaction)
    final_state = 0.5 * flow_state + 0.5 * (
        first + time_step * tendency(extend(first), speeds, viscosity, reaction)
    )
    snapshot = final_state.astype(jnp.bfloat16)
    tile_rows = flow_state.shape[1]
    unit_count = flow_state.shape[2] // YB
    slab_count = lax.axis_size(("grp", "gx"))
    capacity = max(2, 3 * unit_count // slab_count)
    columns = V * YB * NZ
    table_row = lax.dynamic_index_in_dim(
        slab_table[:, :, 0], lax.axis_index("gy"), 0, keepdims=False
    )
    order = jnp.arange(unit_count, dtype=jnp.int32)
    earlier = order[None, :] < order[:, None]
    same_slab = table_row[:, None] == table_row[None, :]
    slot_index = jnp.sum((same_slab & earlier).astype(jnp.int32), axis=1)
    target = table_row * capacity + slot_index
    placing = (
        jnp.arange(slab_count * capacity, dtype=jnp.int32)[:, None] == target[None, :]
    ).astype(jnp.bfloat16)
    blocks = snapshot.reshape(V, tile_rows, unit_count, YB, NZ)
    outgoing = jnp.einsum(
        "pu,vxuyz->pxvyz", placing, blocks, preferred_element_type=jnp.float32
    ).astype(jnp.bfloat16)
    received = lax.all_to_all(
        outgoing.reshape(slab_count, capacity, tile_rows, columns),
        ("grp", "gx"),
        split_axis=0,
        concat_axis=2,
        tiled=True,
    )
    received = received.reshape(capacity, NX, columns)
    partial_value = lax.dot_general(
        received, received, (((0, 2), (0, 2)), ((), ())), preferred_element_type=jnp.float32
    )
    gram = lax.psum(partial_value, ("grp", "gx", "gy"))
    product = jnp.dot(gram, start_basis, precision=lax.Precision.HIGHEST)
    basis = product / jnp.sqrt(jnp.sum(product * product))
    for repeat in range(NEWTON):
        inner_gram = jnp.dot(basis.T, basis, precision=lax.Precision.HIGHEST)
        basis = 1.5 * basis - 0.5 * jnp.dot(basis, inner_gram, precision=lax.Precision.HIGHEST)
    basis_half = basis.astype(jnp.bfloat16)
    cores = jnp.einsum("xr,mxc->mrc", basis_half, received, preferred_element_type=jnp.float32)
    return (final_state, cores.reshape(capacity, R, V, YB, NZ))


def solution(mesh):
    placed = (P(None, ("grp", "gx"), "gy", None), P(), P(), P(), P(), P())
    return jax.shard_map(
        on_device,
        mesh=mesh,
        in_specs=placed,
        out_specs=(
            P(None, ("grp", "gx"), "gy", None),
            P(("grp", "gx", "gy"), None, None, None, None),
        ),
        check_vma=False,
    )
```

profile of v0, /device:TPU:1, one launch (start us, length us, event | category | flops | bytes accessed | tf_op | source)
XLA Modules:
  0.0 519.2 jit_solution(14506563445527793642)
XLA Ops:
  7.2 1.1 fusion.116
  8.3 0.9 copy.103
  9.2 3.0 collective-permute-start.1
  12.2 0.9 copy.104
  13.1 5.8 %fusion.114 = (f32[8,48,16,1]{3,2,1,0:T(8,128)S(1)}, f32[8,48,16,1]{3,2,1,0:T(8,128)}) fusion(f32[8,48,16,128]{3,2,1,0:T(8,128)} %param.6), kind=kLoop, calls=%fused_computation.230 | loop fusion | bytes 98304 | tf_op jit(solution)/shard_map/jit(_roll_static)/slice | solution.py:57
  18.9 3.9 fusion.115
  22.7 1.1 fusion.112
  23.8 3.7 fusion.113
  27.5 1.1 fusion.110
  28.6 1.1 fusion.111
  29.7 1.1 fusion.108
  30.8 1.8 constant_dynamic-update-slice_fusion.3
  32.6 5.7 %constant_dynamic-update-slice_fusion.1 = (f32[8,52,16,128]{3,0,2,1:T(8,128)}, f32[8,52,16,128]{3,0,2,1:T(8,128)}, f32[8,56,16,128]{3,0,2,1:T(8,128)}) fusion(f32[8,48,16,128]{3,2,1,0:T(8,128)S(1)} %copy-done.1, f32[8,52,16,128]{3,0,2,1:T(8,128)} %get-tuple-element.55, f32[8,56,16,128]{3,0,2,1:T(8,128)} %get-tuple-element.56), kind=kLoop, calls=%fused_computation.168 | loop fusion | bytes 12582912
  38.3 0.8 constant_dynamic-update-slice_fusion
  39.2 2.9 fusion.98
  42.0 5.8 %collective-permute-start.2 = (f32[8,56,4,128]{3,0,2,1:T(8,128)}, f32[8,56,4,128]{3,0,2,1:T(8,128)}, u32[]{:S(2)}, u32[]{:S(2)}) collective-permute-start(f32[8,56,4,128]{3,0,2,1:T(8,128)} %get-tuple-element.12), channel_id=1, source_target_pairs={{1,0},{2,1},{3,2},{4,3},{5,4},{6,5},{7,6},{0,7},{9,8},{10,9},{11,1... | collective-permute-start | bytes 2752520 | tf_op jit(solution)/shard_map/ppermute | solution.py:28
  48.0 3.8 fusion.109
  51.8 5.6 %copy.105 = f32[8,48,16,1]{3,0,2,1:T(8,128)} copy(f32[8,48,16,1]{3,2,1,0:T(8,128)} %get-tuple-element.45) | data formatting | bytes 49152
  57.4 3.5 copy.106
  60.9 3.5 copy.107
  64.4 3.5 copy.108
  67.9 3.5 copy.109
  71.5 3.9 copy.110
  75.4 3.4 copy.111
  78.8 3.5 copy.112
  82.3 3.5 copy.113
  85.8 3.4 copy.114
  89.2 3.5 copy.115
  92.7 3.6 copy.116
  96.3 3.5 copy.117
  99.8 3.4 copy.118
  103.3 3.5 copy.119
  106.8 3.4 copy.120
  110.2 0.7 dynamic-slice_bitcast_fusion
  111.1 0.7 multiply_add_fusion
  111.8 37.8 %fusion.43 = f32[8,48,16,128]{3,0,2,1:T(8,128)S(1)} fusion(f32[8,56,16,128]{3,0,2,1:T(8,128)} %get-tuple-element.54, f32[8,56,4,128]{3,0,2,1:T(8,128)} %collective-permute-done.3, f32[8,56,4,128]{3,0,2,1:T(8,128)} %collective-permute-done.2, f32[8,52,16,128]{3,0,2,1:T(8,128)} %get-tuple-element.49, f32[8,52,16,128]{3,0,2,1:T(8,128)} %get-tuple-element.53, ...), kind=kOutput, calls=%fused_computation.70 | convolution fusion | flops 128974848 | bytes 90440736 | tf_op jit(solution)/shard_map/kj,jxyz->kxyz/dot_general | solution.py:42
  149.7 3.8 fusion.99
  153.4 3.8 fusion.100
  157.3 3.8 fusion.101
  161.1 3.9 fusion.102
  165.0 3.8 fusion.103
  168.8 2.8 collective-permute-start.4
  171.5 3.9 fusion.104
  175.4 2.1 collective-permute-done.5
  177.7 5.4 %collective-permute-start.6 = (f32[8,56,4,128]{3,0,2,1:T(8,128)S(1)}, f32[8,56,4,128]{3,0,2,1:T(8,128)S(1)}, u32[]{:S(2)}, u32[]{:S(2)}) collective-permute-start(f32[8,56,4,128]{3,0,2,1:T(8,128)S(1)} %get-tuple-element.10), channel_id=1, source_target_pairs={{1,0},{2,1},{3,2},{4,3},{5,4},{6,5},{7,6},{0,7},{9,8},{10,9},{11,1... | collective-permute-start | bytes 2752520 | tf_op jit(solution)/shard_map/ppermute | solution.py:28
  183.5 3.7 fusion.105
  187.3 3.9 fusion.106
  191.2 9.7 %collective-permute-done.6 = f32[8,56,4,128]{3,0,2,1:T(8,128)S(1)} collective-permute-done((f32[8,56,4,128]{3,0,2,1:T(8,128)S(1)}, f32[8,56,4,128]{3,0,2,1:T(8,128)S(1)}, u32[]{:S(2)}, u32[]{:S(2)}) %collective-permute-start.6) | collective-permute-done | bytes 917536 | tf_op jit(solution)/shard_map/ppermute | solution.py:28
  200.9 5.9 %collective-permute-done.7 = f32[8,56,4,128]{3,0,2,1:T(8,128)S(1)} collective-permute-done((f32[8,56,4,128]{3,0,2,1:T(8,128)S(1)}, f32[8,56,4,128]{3,0,2,1:T(8,128)S(1)}, u32[]{:S(2)}, u32[]{:S(2)}) %collective-permute-start.7) | collective-permute-done | bytes 917536 | tf_op jit(solution)/shard_map/ppermute | solution.py:27
  206.8 3.9 pad_maximum_fusion
  210.7 25.6 %fusion.117 = (bf16[8,48,16,128]{3,0,2,1:T(8,128)(2,1)S(1)}, f32[8,48,16,128]{3,0,2,1:T(8,128)}) fusion(f32[8,48,16,128]{3,0,2,1:T(8,128)S(1)} %fusion.43, f32[8,48,16,124]{3,0,2,1:T(8,128)} %get-tuple-element.16, f32[8,48,16,4]{3,0,2,1:T(8,128)} %get-tuple-element.14, f32[8]{0:T(128)S(1)} %get-tuple-element.62, f32[8,48,16,4]{3,0,2,1:T(8,128)} %get-tuple-element.15, ...), kind=kOutput, calls=%fused_computation.233 | convolution fusion | flops 131334144 | bytes 65028608 | tf_op jit(solution)/shard_map/kj,jxyz->kxyz/dot_general | solution.py:42
  236.4 1.9 convert_bitcast_fusion
  238.3 10.6 %copy.90 = bf16[32,48,8,2,128]{4,3,2,1,0:T(2,128)(2,1)} copy(bf16[32,48,8,2,128]{4,0,3,1,2:T(8,128)(2,1)S(1)} %convert_bitcast_fusion) | data formatting | bytes 12582912 | tf_op jit(solution)/shard_map/convert_element_type | solution.py:91
  248.9 11.1 %reshape.133 = bf16[16,2,48,2048]{3,2,1,0:T(8,128)(2,1)} reshape(bf16[32,48,8,2,128]{4,3,2,1,0:T(2,128)(2,1)} %copy.90) | data formatting | bytes 12582912 | tf_op jit(solution)/shard_map/reshape | solution.py:93
  260.0 78.8 %all_to_all.15 = bf16[16,2,48,2048]{3,2,1,0:T(8,128)(2,1)S(1)} all-to-all(bf16[16,2,48,2048]{3,2,1,0:T(8,128)(2,1)} %reshape.133), channel_id=1, replica_groups=mesh['grp'=4,'gx'=4,'gy'=8] {'grp','gx'}, dimensions={0} | all-to-all | bytes 12582912 | tf_op jit(solution)/shard_map/all_to_all | solution.py:92
  338.8 1.1 copy.91
  339.9 2.7 copy-done.3
  342.6 6.5 %convolution_bitcast_fusion.1 = f32[768,768]{1,0:T(8,128)} fusion(bf16[2,768,2048]{2,1,0:T(8,128)(2,1)S(1)} %bitcast.95), kind=kOutput, calls=%fused_computation.147 | convolution fusion | flops 4831838208 | bytes 8650752 | tf_op jit(solution)/shard_map/dot_general | solution.py:100
  349.1 2.2 copy.92
  351.4 144.7 %all-reduce.2.cloned.1.call-done = f32[768,768]{1,0:T(8,128)} async-done(((f32[768,768]{1,0:T(8,128)}), f32[768,768]{1,0:T(8,128)}) %all-reduce.2.cloned.1.call-update) | async-done | bytes 2359312 | tf_op jit(solution)/shard_map/psum | solution.py:103
  496.1 4.6 multiply_reduce_fusion
  503.5 0.5 fusion.85
  505.7 4.0 convolution_bitcast_fusion
  509.6 2.5 reshape.135
  (56 shorter events, 4.9 us)
Async XLA Ops:
  7.2 488.9 %copy-start = (f32[768,96]{0,1:T(8,128)S(1)}, f32[768,96]{0,1:T(8,128)}, u32[]{:S(2)}) copy-start(f32[768,96]{0,1:T(8,128)} %param.10) | copy-start | bytes 884740
  7.2 488.9 %all-reduce.2.cloned.1.call-start = ((), (), s32[]{:S(2)}) async-start(), calls=%async_computation.1 | async-start | bytes 4718592 | tf_op jit(solution)/shard_map/psum | solution.py:103
  9.2 21.6 %collective-permute-start.1 = (f32[8,4,16,128]{3,0,2,1:T(8,128)}, f32[8,4,16,128]{3,0,2,1:T(8,128)}, u32[]{:S(2)}, u32[]{:S(2)}) collective-permute-start(f32[8,4,16,128]{3,0,2,1:T(8,128)} %copy.103), channel_id=1, source_target_pairs={{0,8},{8,16},{16,24},{24,32},{32,40},{40,48},{48,56},{56,64},{64,7... | collective-permute-start | bytes 786440 | tf_op jit(solution)/shard_map/ppermute | solution.py:27
  13.1 5.8 %copy-start.1 = (f32[8,48,16,128]{3,2,1,0:T(8,128)S(1)}, f32[8,48,16,128]{3,2,1,0:T(8,128)}, u32[]{:S(2)}) copy-start(f32[8,48,16,128]{3,2,1,0:T(8,128)} %param.6) | copy-start | bytes 9437188
  13.1 25.2 %collective-permute-start = (f32[8,4,16,128]{3,0,2,1:T(8,128)}, f32[8,4,16,128]{3,0,2,1:T(8,128)S(1)}, u32[]{:S(2)}, u32[]{:S(2)}) collective-permute-start(f32[8,4,16,128]{3,0,2,1:T(8,128)} %copy.104), channel_id=1, source_target_pairs={{8,0},{16,8},{24,16},{32,24},{40,32},{48,40},{56,48},{64,56},{72,6... | collective-permute-start | bytes 786440 | tf_op jit(solution)/shard_map/ppermute | solution.py:28
  42.0 69.8 %collective-permute-start.2 = (f32[8,56,4,128]{3,0,2,1:T(8,128)}, f32[8,56,4,128]{3,0,2,1:T(8,128)}, u32[]{:S(2)}, u32[]{:S(2)}) collective-permute-start(f32[8,56,4,128]{3,0,2,1:T(8,128)} %get-tuple-element.12), channel_id=1, source_target_pairs={{1,0},{2,1},{3,2},{4,3},{5,4},{6,5},{7,6},{0,7},{9,8},{10,9},{11,1... | collective-permute-start | bytes 2752520 | tf_op jit(solution)/shard_map/ppermute | solution.py:28
  47.8 64.0 %collective-permute-start.3 = (f32[8,56,4,128]{3,0,2,1:T(8,128)}, f32[8,56,4,128]{3,0,2,1:T(8,128)}, u32[]{:S(2)}, u32[]{:S(2)}) collective-permute-start(f32[8,56,4,128]{3,0,2,1:T(8,128)} %get-tuple-element.13), channel_id=1, source_target_pairs={{0,1},{1,2},{2,3},{3,4},{4,5},{5,6},{6,7},{7,0},{8,9},{9,10},{10,1... | collective-permute-start | bytes 2752520 | tf_op jit(solution)/shard_map/ppermute | solution.py:27
  51.8 5.6 %copy-start.7 = (f32[8,48,16,127]{3,2,1,0:T(8,128)S(1)}, f32[8,48,16,127]{3,2,1,0:T(8,128)}, u32[]{:S(2)}) copy-start(f32[8,48,16,127]{3,2,1,0:T(8,128)} %get-tuple-element.47) | copy-start | bytes 9363460
  57.4 3.5 copy-start.6
  67.9 3.6 copy-start.5
  71.5 3.9 copy-start.4
  96.3 3.5 copy-start.9
  99.8 3.4 copy-start.8
  106.8 4.9 copy-start.13
  106.8 4.9 copy-start.14
  106.8 5.0 copy-start.15
  168.8 6.6 %collective-permute-start.4 = (f32[8,4,16,128]{3,0,2,1:T(8,128)S(1)}, f32[8,4,16,128]{3,0,2,1:T(8,128)S(1)}, u32[]{:S(2)}, u32[]{:S(2)}) collective-permute-start(f32[8,4,16,128]{3,0,2,1:T(8,128)S(1)} %get-tuple-element.30), channel_id=1, source_target_pairs={{8,0},{16,8},{24,16},{32,24},{40,32},{48,40},{56,48},{64,56},{72,6... | collective-permute-start | bytes 786440 | tf_op jit(solution)/shard_map/ppermute | solution.py:28
  171.5 6.0 %collective-permute-start.5 = (f32[8,4,16,128]{3,0,2,1:T(8,128)S(1)}, f32[8,4,16,128]{3,0,2,1:T(8,128)S(1)}, u32[]{:S(2)}, u32[]{:S(2)}) collective-permute-start(f32[8,4,16,128]{3,0,2,1:T(8,128)S(1)} %get-tuple-element.31), channel_id=1, source_target_pairs={{0,8},{8,16},{16,24},{24,32},{32,40},{40,48},{48,56},{56,64},{64,7... | collective-permute-start | bytes 786440 | tf_op jit(solution)/shard_map/ppermute | solution.py:27
  175.4 31.4 %copy-start.11 = (f32[8,4,16,128]{3,0,2,1:T(8,128)}, f32[8,4,16,128]{3,0,2,1:T(8,128)S(1)}, u32[]{:S(2)}) copy-start(f32[8,4,16,128]{3,0,2,1:T(8,128)S(1)} %collective-permute-done.4) | copy-start | bytes 786436
  177.6 29.3 %copy-start.12 = (f32[8,4,16,128]{3,0,2,1:T(8,128)}, f32[8,4,16,128]{3,0,2,1:T(8,128)S(1)}, u32[]{:S(2)}) copy-start(f32[8,4,16,128]{3,0,2,1:T(8,128)S(1)} %collective-permute-done.5) | copy-start | bytes 786436
  177.7 23.2 %collective-permute-start.6 = (f32[8,56,4,128]{3,0,2,1:T(8,128)S(1)}, f32[8,56,4,128]{3,0,2,1:T(8,128)S(1)}, u32[]{:S(2)}, u32[]{:S(2)}) collective-permute-start(f32[8,56,4,128]{3,0,2,1:T(8,128)S(1)} %get-tuple-element.10), channel_id=1, source_target_pairs={{1,0},{2,1},{3,2},{4,3},{5,4},{6,5},{7,6},{0,7},{9,8},{10,9},{11,1... | collective-permute-start | bytes 2752520 | tf_op jit(solution)/shard_map/ppermute | solution.py:28
  183.1 23.7 %collective-permute-start.7 = (f32[8,56,4,128]{3,0,2,1:T(8,128)S(1)}, f32[8,56,4,128]{3,0,2,1:T(8,128)S(1)}, u32[]{:S(2)}, u32[]{:S(2)}) collective-permute-start(f32[8,56,4,128]{3,0,2,1:T(8,128)S(1)} %get-tuple-element.11), channel_id=1, source_target_pairs={{0,1},{1,2},{2,3},{3,4},{4,5},{5,6},{6,7},{7,0},{8,9},{9,10},{10,1... | collective-permute-start | bytes 2752520 | tf_op jit(solution)/shard_map/ppermute | solution.py:27
  191.2 19.6 %copy-start.2 = (f32[8,48,16,128]{3,2,1,0:T(8,128)S(1)}, f32[8,48,16,128]{3,2,1,0:T(8,128)}, u32[]{:S(2)}) copy-start(f32[8,48,16,128]{3,2,1,0:T(8,128)} %param.6) | copy-start | bytes 9437188
  339.9 2.7 copy-start.3
  342.6 6.5 %copy-start.10 = (f32[8,48,16,128]{3,0,2,1:T(8,128)S(1)}, f32[8,48,16,128]{3,0,2,1:T(8,128)}, u32[]{:S(2)}) copy-start(f32[8,48,16,128]{3,0,2,1:T(8,128)} %get-tuple-element.83) | copy-start | bytes 9437188
Sparse Core Ops, SparseCore 0:
  349.3 146.7 all-reduce.1
where the time goes:
time: 528 us; the launch traced here: 519 us
  waiting for transfers between devices  163 us (31%)
  local copies, waits for them, and re-layouts  155 us (29%)
  matrix products  84.6 us (16%)
  blocking collectives  78.8 us (15%)
  starting transfers between devices  17.6 us (3%)
  between operations  15.2 us (3%)
    psum x1, waiting for transfers between devices, on_device(): gram = lax.psum(partial_value, ('grp', 'gx', 'gy'))  145 us
    all_to_all x1, blocking collectives, on_device(): lax.all_to_all(outgoing.reshape(slab_count, capacity, tile_rows, columns)...  78.8 us
    unnamed x53, local copies, waits for them, and re-layouts  72.6 us
    dot_general x2, matrix products, tendency(): jnp.einsum('kj,jxyz->kxyz', reaction, center, precision=lax.Precision.HIG...  63.4 us
    slice x16, local copies, waits for them, and re-layouts, tendency(): jnp.roll(center, offset, 3)  52 us
    ppermute x4, starting transfers between devices, extended(): after = lax.ppermute(initial, axis, down)  13.9 us
    reshape x1, local copies, waits for them, and re-layouts, on_device(): outgoing.reshape(slab_count, capacity, tile_rows, columns)  11.1 us
    convert_element_type x1, local copies, waits for them, and re-layouts, on_device(): outgoing = jnp.einsum('pu,vxuyz->pxvyz', placing, blocks, preferred_eleme...  10.6 us
  transfers between devices with their start and end apart: 9, of which 4 were waited for; matrix products, arithmetic and copies ran while one was open for 20% of the time, Pallas kernels for 0%

commit v1 on v0

v1 whole, which is shorter than its diff:
```python
import jax
import jax.numpy as jnp
from jax import lax
from jax.experimental import pallas as pl
from jax.experimental.pallas import tpu as pltpu
from jax.sharding import PartitionSpec as P

V = 8
NX = 768
R = 96
RP = 128
NZ = 128
TX = 48
TY = 16
TILES = 16
ROWS = 8
UNITS = 8
MOST = 2
NEWTON = 5
CH = 16
CHUNKS = TX // CH
CHUNK_ORDER = (0, 2, 1)
EARLY = (2, 3, 4, 5)
LATE = (0, 1, 6, 7)
UNIT_ORDER = EARLY + LATE

slope_weights = (0.8, -0.2, 4.0 / 105.0, -1.0 / 280.0)
curve_weights = (1.6, -0.2, 8.0 / 315.0, -1.0 / 560.0)
curve_center = -205.0 / 72.0
time_step = 0.2

MESH = pl.DeviceIdType.MESH
F32 = jnp.float32
BF16 = jnp.bfloat16
NT = (((1,), (1,)), ((), ()))


def split(x):
    high = x.astype(BF16)
    return high, (x - high.astype(F32)).astype(BF16)


def mm(a, b):
    return jnp.dot(a, b, preferred_element_type=F32)


def mm_nt(a, b):
    return lax.dot_general(a, b, NT, preferred_element_type=F32)


def both(a, b):

    ah, al = split(a)
    bh, bl = split(b)
    left = jnp.concatenate([ah, ah, al], axis=1)
    right = jnp.concatenate([bh, bl, bh], axis=0)
    return mm(left, right)


def iota(shape, dim):
    return lax.broadcasted_iota(jnp.int32, shape, dim)


def curve_of(distance):
    out = jnp.zeros(distance.shape, F32)
    for m in range(1, 5):
        hit = (distance == m) | (distance == -m)
        out = jnp.where(hit, time_step * curve_weights[m - 1], out)
    return out


def slope_of(distance):
    out = jnp.zeros(distance.shape, F32)
    for m in range(1, 5):
        out = jnp.where(distance == m, -time_step * slope_weights[m - 1], out)
        out = jnp.where(distance == -m, time_step * slope_weights[m - 1], out)
    return out


def kernel(
    flow_hbm, speeds, viscosity, reaction, start_ref, table,
    final_hbm, core_hbm,
    e1, e2, acc,
    ylo_out, yhi_out, ylo_in, yhi_in,
    xlo_out, xhi_out, xlo_in, xhi_in,
    sbuf, srec,
    cz, wy, wh,
    start_t, pacc, psend, prec, qrec, pfull, prod_t, blocks, csend, crec,
    picks,
    load_sem, final_sem, core_sem,
    y_send, y_recv, x_send, x_recv, s_send, s_recv, s_own,
    p_send, p_recv, q_send, q_recv, f_send, f_recv, c_send, c_recv,
):
    grp, gx, gy = (lax.axis_index(a) for a in ("grp", "gx", "gy"))
    me = grp * 4 + gx

    def tile(i):
        return (lax.div(i, 4), lax.rem(i, 4), gy)

    def row(i):
        return (grp, gx, i)

    def wrap(i, n):
        return lax.rem(i, n)

    barrier = pltpu.get_barrier_semaphore()

    @pl.loop(1, TILES)
    def _(d):
        pl.semaphore_signal(barrier, inc=1, device_id=tile(wrap(me + d, TILES)), device_id_type=MESH)

    @pl.loop(1, ROWS)
    def _(d):
        pl.semaphore_signal(barrier, inc=1, device_id=row(wrap(gy + d, ROWS)), device_id_type=MESH)

    load = pltpu.make_async_copy(flow_hbm, e1.at[:, 4 : 4 + TX], load_sem)
    load.start()

    square = (128, 128)
    turn = (iota(square, 0) - iota(square, 1)) & 127
    turn = jnp.where(turn > 64, turn - 128, turn)
    z_curve, z_slope = curve_of(turn), slope_of(turn)
    y_shape = (TY, 128)
    y_dist = (iota(y_shape, 1) & 15) - iota(y_shape, 0)
    y_var = lax.shift_right_logical(iota(y_shape, 1), 4)
    y_curve = jnp.where(y_dist == 0, time_step * 3.0 * curve_center, curve_of(y_dist))
    y_slope = slope_of(y_dist)
    h_shape = (TY, 64)
    h_col = iota(h_shape, 1)
    h_dist = (h_col & 3) - 4 + lax.shift_right_logical(h_col, 5) * 20 - iota(h_shape, 0)
    h_var = lax.shift_right_logical(h_col, 2) & 7
    h_curve, h_slope = curve_of(h_dist), slope_of(h_dist)

    @pl.loop(0, V)
    def _(k):
        v, s2, s3 = viscosity[k], speeds[1, k], speeds[2, k]
        ch, cl = split(v * z_curve + s3 * z_slope)
        cz[k] = jnp.concatenate(
            [jnp.concatenate([ch, cl], axis=1), jnp.concatenate([ch, jnp.zeros_like(cl)], axis=1)], axis=0
        )
        w = jnp.where(y_var == k, v * y_curve + s2 * y_slope, 0.0)
        for j in range(V):
            w = w + jnp.where((y_var == j) & (y_dist == 0), time_step * reaction[k, j], 0.0)
        hi, lo = split(w)
        at = pl.ds(pl.multiple_of(k * TY, TY), TY)
        at2 = pl.ds(pl.multiple_of(128 + k * TY, TY), TY)
        wy[at, :] = jnp.concatenate([hi, hi], axis=1)
        wy[at2, :] = jnp.concatenate([lo, jnp.zeros_like(lo)], axis=1)
        hi, lo = split(jnp.where(h_var == k, v * h_curve + s2 * h_slope, 0.0))
        wh[at, :] = hi
        wh[at2, :] = lo

    f_row, f_col = iota((64, 128), 0), iota((64, 128), 1)
    f_src = (lax.shift_right_logical(f_row, 2) & 7) * 16 + (f_row & 3) + lax.shift_right_logical(f_row, 5) * 12
    face = (f_src == f_col).astype(BF16)

    q_row, q_col = iota((128, 256), 0), iota((128, 256), 1)
    q_unit = lax.shift_right_logical(q_row, 4) & 3
    q_par = lax.shift_right_logical(q_row, 6)
    q_base = (q_row & 15) * 16 + q_par
    pick_early = (q_base + 2 * (q_unit + 2) == q_col).astype(BF16)
    pick_late = (q_base + 2 * jnp.where(q_unit < 2, q_unit, q_unit + 4) == q_col).astype(BF16)

    for p in range(TILES):
        count = jnp.int32(0)
        place = [jnp.int32(0)] * MOST
        valid = [jnp.int32(0)] * MOST
        for u in range(UNITS):
            hit = table[gy, u, 0] == p
            for m in range(MOST):
                take = hit & (count == m)
                place[m] = jnp.where(take, UNIT_ORDER.index(u), place[m])
                valid[m] = jnp.where(take, 1, valid[m])
            count = count + hit.astype(jnp.int32)
        for m in range(MOST):
            picks[p, m] = place[m]
            picks[p, MOST + m] = valid[m]

    pfull[...] = jnp.zeros((NX, RP), F32)
    pfull[:, 0:R] = start_ref[...]
    eye = (iota(square, 0) == iota(square, 1)).astype(BF16)
    hi, lo = split(pfull[...])
    start_t[0:RP, :] = mm_nt(eye, hi).astype(BF16)
    start_t[RP:, :] = mm_nt(eye, lo).astype(BF16)

    def y_copy(stage, side, c):
        at = pl.ds(c * CH, CH)
        out, into = (ylo_out, yhi_in) if side == 0 else (yhi_out, ylo_in)
        peer = row(wrap(gy + (ROWS - 1 if side == 0 else 1), ROWS))
        return pltpu.make_async_remote_copy(
            src_ref=out.at[stage, at], dst_ref=into.at[stage, at],
            send_sem=y_send.at[stage, side, c], recv_sem=y_recv.at[stage, side, c],
            device_id=peer, device_id_type=MESH,
        )

    def x_copy(stage, side):
        out, into = (xlo_out, xhi_in) if side == 0 else (xhi_out, xlo_in)
        peer = tile(wrap(me + (TILES - 1 if side == 0 else 1), TILES))
        return pltpu.make_async_remote_copy(
            src_ref=out.at[stage], dst_ref=into.at[stage],
            send_sem=x_send.at[stage, side], recv_sem=x_recv.at[stage, side],
            device_id=peer, device_id_type=MESH,
        )

    def pack_faces(stage, x, rows):
        faces = mm(face, rows.astype(BF16)).astype(BF16)
        for i in range(2):
            part = faces[:, i * 128 : (i + 1) * 128]
            ylo_out[stage, x + i] = part[0:32]
            yhi_out[stage, x + i] = part[32:64]

    def pair(ref, x):
        return jnp.concatenate([ref[:, x].reshape(128, 128), ref[:, x + 1].reshape(128, 128)], axis=1)

    def send_x(stage, e):
        xlo_out[stage] = e[:, 4:8].astype(BF16)
        xhi_out[stage] = e[:, TX : TX + 4].astype(BF16)
        for side in range(2):
            x_copy(stage, side).start()

    def receive_x(stage, e):
        for side in range(2):
            x_copy(stage, side).wait_recv()
        e[:, 0:4] = xlo_in[stage].astype(F32)
        e[:, TX + 4 : TX + 8] = xhi_in[stage].astype(F32)

    def along_xz(e, out, at, k, x):
        here = e[k, pl.ds(x + 4, 8)]
        hi, lo = split(here.reshape(128, 128))
        res = mm(jnp.concatenate([hi, lo], axis=1), cz[k])
        total = here + (res[:, 0:128] + res[:, 128:]).reshape(8, TY, NZ)
        v, s1 = viscosity[k], speeds[0, k]
        for m in range(1, 5):
            b, a = time_step * curve_weights[m - 1] * v, time_step * slope_weights[m - 1] * s1
            total = total + (b - a) * e[k, pl.ds(x + 4 + m, 8)] + (b + a) * e[k, pl.ds(x + 4 - m, 8)]
        out[k, pl.ds(x + at, 8)] = total

    def along_y(e, out, at):
        @pl.loop(0, TX // 2)
        def _(i):
            x = i * 2
            hi, lo = split(pair(e, x + 4))
            res = mm(wy[...], jnp.concatenate([hi, lo], axis=0))
            res = res[0:128] + res[128:]
            for n in range(2):
                out[:, x + at + n] = out[:, x + at + n] + res[:, n * 128 : (n + 1) * 128].reshape(V, TY, NZ)

    def from_halo(stage, x):
        rhs = jnp.concatenate(
            [jnp.concatenate([ylo_in[stage, x + n], yhi_in[stage, x + n]], axis=0) for n in range(2)], axis=1
        )
        res = mm(wh[...], rhs)
        return res[0:128] + res[128:]

    def bulk(stage, e, out, at):
        @pl.loop(0, V)
        def _(k):
            @pl.loop(1, TX // 8 - 1)
            def _(c):
                along_xz(e, out, at, k, c * 8)

        along_y_first = stage == 0
        if along_y_first:
            pass
        receive_x(stage, e)

        @pl.loop(0, V)
        def _(k):
            along_xz(e, out, at, k, 0)
            along_xz(e, out, at, k, TX - 8)

        along_y(e, out, at)

    load.wait()
    pl.semaphore_wait(barrier, TILES - 1 + ROWS - 1)
    send_x(0, e1)
    for c in CHUNK_ORDER:
        @pl.loop(0, CH // 2)
        def _(i):
            x = c * CH + i * 2
            pack_faces(0, x, pair(e1, x + 4))

        for side in range(2):
            y_copy(0, side, c).start()

    bulk(0, e1, e2, 4)
    for n, c in enumerate(CHUNK_ORDER):
        for side in range(2):
            y_copy(0, side, c).wait_recv()

        @pl.loop(0, CH // 2)
        def _(i):
            x = c * CH + i * 2
            rows = pair(e2, x + 4) + from_halo(0, x)
            for j in range(2):
                e2[:, x + 4 + j] = rows[:, j * 128 : (j + 1) * 128].reshape(V, TY, NZ)
            pack_faces(1, x, rows)

        for side in range(2):
            y_copy(1, side, c).start()
        if n == 1:
            send_x(1, e2)

    bulk(1, e2, acc, 0)

    def order_lines(pick, part):
        @pl.loop(0, V)
        def _(k):
            for g in range(TX // 16):
                at = pl.ds(g * 16, 16)
                lines = acc[k, at]
                if part == 0:
                    lines = 0.5 * (e1[k, pl.ds(g * 16 + 4, 16)] + lines)
                    acc[k, at] = lines
                got = mm(pick, lines.reshape(256, NZ).astype(BF16)).astype(BF16)
                for j in range(2):
                    for u in range(4):
                        r = (j * 4 + u) * 16
                        lane = part * 512 + u * 128
                        sbuf[k, j, g * 16 : g * 16 + 16, lane : lane + 128] = got[r : r + 16]

    def s_copy(part, d):
        peer = wrap(me + d, TILES)
        lanes = pl.ds(part * 512, 512)
        return pltpu.make_async_remote_copy(
            src_ref=sbuf.at[lax.div(peer, 2), lax.rem(peer, 2), :, lanes],
            dst_ref=srec.at[pl.ds(pl.multiple_of(me * TX, TX), TX), lanes],
            send_sem=s_send.at[part, d], recv_sem=s_recv.at[part, d],
            device_id=tile(peer), device_id_type=MESH,
        )

    def s_arrival(part, d):
        source = wrap(me + TILES - d, TILES)
        lanes = pl.ds(part * 512, 512)
        return pltpu.make_async_remote_copy(
            src_ref=sbuf.at[0, 0, :, lanes],
            dst_ref=srec.at[pl.ds(pl.multiple_of(source * TX, TX), TX), lanes],
            send_sem=s_send.at[part, d], recv_sem=s_recv.at[part, d],
            device_id=tile(source), device_id_type=MESH,
        )

    def s_local(part):
        lanes = pl.ds(part * 512, 512)
        return pltpu.make_async_copy(
            sbuf.at[lax.div(me, 2), lax.rem(me, 2), :, lanes],
            srec.at[pl.ds(pl.multiple_of(me * TX, TX), TX), lanes],
            s_own.at[part],
        )

    def send_lines(part):
        @pl.loop(1, TILES)
        def _(d):
            s_copy(part, d).start()

        s_local(part).start()

    def receive_lines(part):
        @pl.loop(1, TILES)
        def _(d):
            s_arrival(part, d).wait_recv()

        s_local(part).wait()

    def add_product(part):
        lanes = slice(part * 512, part * 512 + 512)
        res = mm(start_t[...], srec[:, lanes])
        hi, lo = split(res[0:RP] + res[RP:])
        right = jnp.concatenate([hi, lo], axis=0)

        @pl.loop(0, NX // 128)
        def _(i):
            at = pl.ds(pl.multiple_of(i * 128, 128), 128)
            got = mm_nt(srec[at, lanes], right)
            got = got[:, 0:RP] + got[:, RP:]
            if part == 0:
                pacc[at, :] = got
            else:
                got = pacc[at, :] + got
                pacc[at, :] = got
                psend[at, :] = got.astype(BF16)

    order_lines(pick_early, 0)
    send_lines(0)
    for c in CHUNK_ORDER:
        for side in range(2):
            y_copy(1, side, c).wait_recv()

        @pl.loop(0, CH // 2)
        def _(i):
            x = c * CH + i * 2
            rows = 0.5 * from_halo(1, x)
            for j in range(2):
                acc[:, x + j] = acc[:, x + j] + rows[:, j * 128 : (j + 1) * 128].reshape(V, TY, NZ)

    order_lines(pick_late, 1)
    send_lines(1)
    store = pltpu.make_async_copy(acc, final_hbm, final_sem)
    store.start()

    receive_lines(0)
    add_product(0)
    receive_lines(1)
    add_product(1)

    def p_copy(d, peer, source):
        return pltpu.make_async_remote_copy(
            src_ref=psend.at[pl.ds(pl.multiple_of(peer * TX, TX), TX)], dst_ref=prec.at[source],
            send_sem=p_send.at[d], recv_sem=p_recv.at[d], device_id=tile(peer), device_id_type=MESH,
        )

    mine = pl.ds(pl.multiple_of(me * TX, TX), TX)

    @pl.loop(1, TILES)
    def _(d):
        p_copy(d, wrap(me + d, TILES), me).start()

    prec[me] = psend[mine, :]

    @pl.loop(1, TILES)
    def _(d):
        p_copy(d, me, wrap(me + TILES - d, TILES)).wait_recv()

    total = prec[0].astype(F32)
    for i in range(1, TILES):
        total = total + prec[i].astype(F32)
    qrec[gy] = total

    def q_copy(d, peer, source):
        return pltpu.make_async_remote_copy(
            src_ref=qrec.at[gy], dst_ref=qrec.at[source],
            send_sem=q_send.at[d], recv_sem=q_recv.at[d], device_id=row(peer), device_id_type=MESH,
        )

    @pl.loop(1, ROWS)
    def _(d):
        q_copy(d, wrap(gy + d, ROWS), gy).start()

    @pl.loop(1, ROWS)
    def _(d):
        q_copy(d, gy, wrap(gy + ROWS - d, ROWS)).wait_recv()

    total = qrec[0]
    for i in range(1, ROWS):
        total = total + qrec[i]
    pfull[mine, :] = total

    def f_copy(d, peer, source):
        return pltpu.make_async_remote_copy(
            src_ref=pfull.at[mine], dst_ref=pfull.at[pl.ds(pl.multiple_of(source * TX, TX), TX)],
            send_sem=f_send.at[d], recv_sem=f_recv.at[d], device_id=tile(peer), device_id_type=MESH,
        )

    @pl.loop(1, TILES)
    def _(d):
        f_copy(d, wrap(me + d, TILES), me).start()

    @pl.loop(1, TILES)
    def _(d):
        f_copy(d, me, wrap(me + TILES - d, TILES)).wait_recv()

    product = pfull[...]
    turned = product.T
    prod_t[...] = turned
    norm = jnp.sum(jnp.sum(product * product, axis=0, keepdims=True), axis=1, keepdims=True)
    hi, lo = split(turned)
    inner = mm_nt(hi, hi) + (mm_nt(hi, lo) + mm_nt(lo, hi))
    inner = inner / norm
    ident = (iota(square, 0) == iota(square, 1)).astype(F32)
    chain = None
    for n in range(NEWTON):
        factor = 1.5 * ident - 0.5 * inner
        chain = factor if n == 0 else both(factor, chain)
        if n < NEWTON - 1:
            inner = both(factor, both(inner, factor))
    basis_t = both(chain, prod_t[...]) / jnp.sqrt(norm)
    half = basis_t.astype(BF16)
    for u in range(UNITS):
        got = mm(half, srec[:, u * 128 : (u + 1) * 128])
        blocks[u] = got[0:R].astype(BF16)

    @pl.loop(0, TILES)
    def _(p):
        for m in range(MOST):
            got = blocks[picks[p, m]]
            csend[p, m] = jnp.where(picks[p, MOST + m] == 1, got, jnp.zeros_like(got))

    def c_copy(d, peer, source):
        return pltpu.make_async_remote_copy(
            src_ref=csend.at[peer], dst_ref=crec.at[source],
            send_sem=c_send.at[d], recv_sem=c_recv.at[d], device_id=tile(peer), device_id_type=MESH,
        )

    @pl.loop(1, TILES)
    def _(d):
        c_copy(d, wrap(me + d, TILES), me).start()

    crec[me] = csend[me]

    @pl.loop(1, TILES)
    def _(d):
        c_copy(d, me, wrap(me + TILES - d, TILES)).wait_recv()

    out = pltpu.make_async_copy(crec, core_hbm, core_sem)
    out.start()

    for stage in range(2):
        for side in range(2):
            x_copy(stage, side).wait_send()
            for c in range(CHUNKS):
                y_copy(stage, side, c).wait_send()

    @pl.loop(1, TILES)
    def _(d):
        peer = wrap(me + d, TILES)
        for part in range(2):
            s_copy(part, d).wait_send()
        p_copy(d, peer, me).wait_send()
        f_copy(d, peer, me).wait_send()
        c_copy(d, peer, me).wait_send()

    @pl.loop(1, ROWS)
    def _(d):
        q_copy(d, wrap(gy + d, ROWS), gy).wait_send()

    store.wait()
    out.wait()


def unpack(core_ref, out_ref):
    for m in range(MOST):
        for s in range(TILES):
            out_ref[m, :, s, :] = core_ref[s, m].astype(F32)


def on_device(flow_state, speeds, viscosity, reaction, start_basis, slab_table):
    dma = pltpu.SemaphoreType.DMA
    vmem = pltpu.VMEM
    halo_y = vmem((2, TX, 32, NZ), BF16)
    halo_x = vmem((2, V, 4, TY, NZ), BF16)
    hbm = pl.BlockSpec(memory_space=pl.ANY)
    smem = pl.BlockSpec(memory_space=pltpu.SMEM)
    final_state, cores = pl.pallas_call(
        kernel,
        name="sections_and_core",
        out_shape=(
            jax.ShapeDtypeStruct((V, TX, TY, NZ), F32),
            jax.ShapeDtypeStruct((TILES, MOST, R, NZ), BF16),
        ),
        in_specs=[hbm, smem, smem, smem, pl.BlockSpec(memory_space=pltpu.VMEM), smem],
        out_specs=(hbm, hbm),
        scratch_shapes=[
            vmem((V, TX + 8, TY, NZ), F32),
            vmem((V, TX + 8, TY, NZ), F32),
            vmem((V, TX, TY, NZ), F32),
            halo_y, halo_y, halo_y, halo_y,
            halo_x, halo_x, halo_x, halo_x,
            vmem((V, 2, TX, UNITS * NZ), BF16),
            vmem((NX, UNITS * NZ), BF16),
            vmem((V, 256, 256), BF16),
            vmem((256, 256), BF16),
            vmem((256, 64), BF16),
            vmem((2 * RP, NX), BF16),
            vmem((NX, RP), F32),
            vmem((NX, RP), BF16),
            vmem((TILES, TX, RP), BF16),
            vmem((ROWS, TX, RP), F32),
            vmem((NX, RP), F32),
            vmem((RP, NX), F32),
            vmem((UNITS, R, NZ), BF16),
            vmem((TILES, MOST, R, NZ), BF16),
            vmem((TILES, MOST, R, NZ), BF16),
            pltpu.SMEM((TILES, 2 * MOST), jnp.int32),
            dma(()), dma(()), dma(()),
            dma((2, 2, CHUNKS)), dma((2, 2, CHUNKS)), dma((2, 2)), dma((2, 2)),
            dma((2, TILES)), dma((2, TILES)), dma((2,)),
            dma((TILES,)), dma((TILES,)), dma((ROWS,)), dma((ROWS,)),
            dma((TILES,)), dma((TILES,)), dma((TILES,)), dma((TILES,)),
        ],
        compiler_params=pltpu.CompilerParams(
            collective_id=0, has_side_effects=True, vmem_limit_bytes=56 * 1024 * 1024
        ),
    )(flow_state, speeds, viscosity, reaction, start_basis, slab_table)
    core_slots = pl.pallas_call(
        unpack,
        name="unpack_core",
        out_shape=jax.ShapeDtypeStruct((MOST, R, TILES, NZ), F32),
        in_specs=[pl.BlockSpec(memory_space=pltpu.VMEM)],
        out_specs=pl.BlockSpec(memory_space=pltpu.VMEM),
        compiler_params=pltpu.CompilerParams(vmem_limit_bytes=32 * 1024 * 1024),
    )(cores)
    return final_state, core_slots.reshape(MOST, R, V, 2, NZ)


def solution(mesh):
    field = P(None, ("grp", "gx"), "gy", None)
    return jax.shard_map(
        on_device,
        mesh=mesh,
        in_specs=(field, P(), P(), P(), P(), P()),
        out_specs=(field, P(("grp", "gx", "gy"), None, None, None, None)),
        check_vma=False,
    )
```

time: 528 us -> 116 us (0.22); the launches traced: 519 us -> 115 us
  waiting for transfers between devices: 163 us -> 0 us
  local copies, waits for them, and re-layouts: 155 us -> 8.17 us
  Pallas kernels: 0 us -> 106 us
  matrix products: 84.6 us -> 0 us
  blocking collectives: 78.8 us -> 0 us
  starting transfers between devices: 17.6 us -> 0 us
  between operations: 15.2 us -> 0.65 us
    psum x1 -> x0, waiting for transfers between devices: 145 us -> none  [on_device(): gram = lax.psum(partial_value, ('grp', 'gx', 'gy'))]
    pallas_call x0 -> x2, Pallas kernels: none -> 106 us  [the longest x1 104 us: on_device(): pl.pallas_call(kernel, name='sections_and_core', out_shape=(jax.ShapeDtyp...]
    dot_general x16 -> x0, matrix products: 84.6 us -> none  [the longest x2 63.4 us: tendency(): jnp.einsum('kj,jxyz->kxyz', reaction, center, precision=lax.Precision.HIG...]
    all_to_all x1 -> x0, blocking collectives: 78.8 us -> none  [on_device(): lax.all_to_all(outgoing.reshape(slab_count, capacity, tile_rows, columns)...]
    unnamed x53 -> x5, local copies, waits for them, and re-layouts: 72.6 us -> 8.17 us
    slice x19 -> x0, local copies, waits for them, and re-layouts: 56 us -> none  [the longest x16 52 us: tendency(): jnp.roll(center, offset, 3)]
    ppermute x8 -> x0, waiting for transfers between devices: 17.8 us -> none  [the longest x4 9.75 us: extended(): after = lax.ppermute(initial, axis, down)]
    ppermute x8 -> x0, starting transfers between devices: 17.6 us -> none  [the longest x4 13.9 us: extended(): after = lax.ppermute(initial, axis, down)]
  transfers between devices with their start and end apart: 9 -> 0, of which waited for: 4 -> 0; matrix products, arithmetic and copies ran while one was open for 20% -> 0% of each run, Pallas kernels for 0% -> 0%
where the time goes in v1:
time: 116 us; the launch traced here: 115 us
  Pallas kernels  106 us (91%)
  local copies, waits for them, and re-layouts  8.17 us (7%)
    pallas_call x1, Pallas kernels, on_device(): pl.pallas_call(kernel, name='sections_and_core', out_shape=(jax.ShapeDtyp...  104 us
    unnamed x5, local copies, waits for them, and re-layouts  8.17 us

profile of v1, /device:TPU:1, one launch (start us, length us, event | category | flops | bytes accessed | tf_op | source)
XLA Modules:
  0.0 115.2 jit_solution(17789160632802598867)
XLA Ops:
  0.6 1.4 %copy.9.table = s32[8,8,1]{2,1,0:T(8,128)} copy(s32[8,8,1]{1,2,0:T(1,128)} %param.11) | data formatting | bytes 512 | tf_op args[5]
  2.0 1.9 %copy.8.start_ref = f32[768,96]{1,0:T(8,128)} copy(f32[768,96]{0,1:T(8,128)} %param.10) | data formatting | bytes 589824 | tf_op args[4]
  3.9 104.3 %sections_and_core.1 = (f32[8,48,16,128]{3,2,1,0:T(8,128)}, bf16[16,2,96,128]{3,2,1,0:T(8,128)(2,1)}) custom-call(f32[8,48,16,128]{3,2,1,0:T(8,128)} %flow_hbm.1, f32[3,8]{1,0:T(4,128)} %speeds.1, f32[8]{0:T(128)} %viscosity.1, f32[8,8]{1,0:T(8,128)} %reaction.1, f32[768,96]{1,0:T(8,128)} %copy.8.start_ref, s32[8,8,1]{2,1,0:T(8,128)} %copy.9.table), custom_call_target="tpu_custom_call" | custom-call | tf_op jit(solution)/shard_map/sections_and_core/pallas_call | solution.py:542
  108.2 0.0 copy-start
  108.2 1.1 copy-done
  109.3 2.1 %unpack_core.1 = f32[2,96,16,128]{3,2,1,0:T(8,128)} custom-call(bf16[16,2,96,128]{3,2,1,0:T(8,128)(2,1)S(1)} %copy-done), custom_call_target="tpu_custom_call" | custom-call | tf_op jit(solution)/shard_map/unpack_core/pallas_call | solution.py:583
  111.5 3.8 %copy.11 = f32[8,48,16,128]{3,2,1,0:T(8,128)} copy(f32[8,48,16,128]{3,2,1,0:T(8,128)} %get-tuple-element.8) | data formatting | bytes 6291456
Async XLA Ops:
  108.2 1.1 copy-start

commit v2 on v1

v2 whole, which is shorter than its diff:
```python
import jax
import jax.numpy as jnp
from jax import lax
from jax.experimental import pallas as pl
from jax.experimental.pallas import tpu as pltpu
from jax.sharding import PartitionSpec as P

V = 8
NX = 768
R = 96
RP = 128
NZ = 128
TX = 48
TY = 16
TILES = 16
ROWS = 8
UNITS = 8
MOST = 2
NEWTON = 5
CH = 16
CHUNKS = TX // CH
CHUNK_ORDER = (1, 0, 2)
PEERS = (
    (2, 1, 0), (1, 0, 0), (3, 0, 0), (0, 1, 0), (2, 1, 1), (1, 0, 1), (3, 0, 1), (0, 1, 1),
    (2, 0, 0), (1, 1, 0), (3, 1, 0), (2, 0, 1), (1, 1, 1), (3, 1, 1), (0, 0, 1),
)
SAME_CORE = tuple(n for n in range(15) if PEERS[n][2] == 0)
PARTNER = 14
EARLY = (2, 3, 4, 5)
LATE = (0, 1, 6, 7)
UNIT_ORDER = EARLY + LATE

slope_weights = (0.8, -0.2, 4.0 / 105.0, -1.0 / 280.0)
curve_weights = (1.6, -0.2, 8.0 / 315.0, -1.0 / 560.0)
curve_center = -205.0 / 72.0
time_step = 0.2

MESH = pl.DeviceIdType.MESH
F32 = jnp.float32
BF16 = jnp.bfloat16
NT = (((1,), (1,)), ((), ()))


def split(x):
    high = x.astype(BF16)
    return high, (x - high.astype(F32)).astype(BF16)


def mm(a, b):
    return jnp.dot(a, b, preferred_element_type=F32)


def mm_nt(a, b):
    return lax.dot_general(a, b, NT, preferred_element_type=F32)


def both(a, b):

    ah, al = split(a)
    bh, bl = split(b)
    left = jnp.concatenate([ah, ah, al], axis=1)
    right = jnp.concatenate([bh, bl, bh], axis=0)
    return mm(left, right)


def iota(shape, dim):
    return lax.broadcasted_iota(jnp.int32, shape, dim)


def curve_of(distance):
    out = jnp.zeros(distance.shape, F32)
    for m in range(1, 5):
        hit = (distance == m) | (distance == -m)
        out = jnp.where(hit, time_step * curve_weights[m - 1], out)
    return out


def slope_of(distance):
    out = jnp.zeros(distance.shape, F32)
    for m in range(1, 5):
        out = jnp.where(distance == m, -time_step * slope_weights[m - 1], out)
        out = jnp.where(distance == -m, time_step * slope_weights[m - 1], out)
    return out


def kernel(
    flow_hbm, speeds, viscosity, reaction, start_ref, table,
    acc, crec,
    e1, e2,
    ylo_out, yhi_out, ylo_in, yhi_in,
    xlo_out, xhi_out, xlo_in, xhi_in,
    sbuf, srec,
    cz, wy, wh,
    start_t, pacc, psend, prec, qrec, pfull, prod_t, blocks, csend,
    picks,
    load_sem,
    y_send, y_recv, x_send, x_recv, s_send, s_recv,
    p_send, p_recv, q_send, q_recv, f_send, f_recv, g_send, g_recv, c_send, c_recv,
):
    grp, gx, gy = (lax.axis_index(a) for a in ("grp", "gx", "gy"))
    me = grp * 4 + gx

    def tile(i):
        return (lax.div(i, 4), lax.rem(i, 4), gy)

    def tile_at(n, back=False):
        dg, dz, dc = PEERS[n]
        g = lax.rem(grp + (4 - dg if back else dg), 4)
        x = lax.rem(lax.div(gx, 2) + dz, 2) * 2 + lax.rem(gx + dc, 2)
        return g, x, g * 4 + x

    def row(i):
        return (grp, gx, i)

    def wrap(i, n):
        return lax.rem(i, n)

    barrier = pltpu.get_barrier_semaphore()

    @pl.loop(1, TILES)
    def _(d):
        pl.semaphore_signal(barrier, inc=1, device_id=tile(wrap(me + d, TILES)), device_id_type=MESH)

    @pl.loop(1, ROWS)
    def _(d):
        pl.semaphore_signal(barrier, inc=1, device_id=row(wrap(gy + d, ROWS)), device_id_type=MESH)

    load = pltpu.make_async_copy(flow_hbm, e1.at[:, 4 : 4 + TX], load_sem)
    load.start()

    f_row, f_col = iota((64, 128), 0), iota((64, 128), 1)
    f_src = (lax.shift_right_logical(f_row, 2) & 7) * 16 + (f_row & 3) + lax.shift_right_logical(f_row, 5) * 12
    face = (f_src == f_col).astype(BF16)

    q_row, q_col = iota((128, 256), 0), iota((128, 256), 1)
    q_unit = lax.shift_right_logical(q_row, 4) & 3
    q_par = lax.shift_right_logical(q_row, 6)
    q_base = (q_row & 15) * 16 + q_par
    pick_early = (q_base + 2 * (q_unit + 2) == q_col).astype(BF16)
    pick_late = (q_base + 2 * jnp.where(q_unit < 2, q_unit, q_unit + 4) == q_col).astype(BF16)

    def y_copy(stage, side):
        out, into = (ylo_out, yhi_in) if side == 0 else (yhi_out, ylo_in)
        peer = row(wrap(gy + (ROWS - 1 if side == 0 else 1), ROWS))
        return pltpu.make_async_remote_copy(
            src_ref=out.at[stage], dst_ref=into.at[stage],
            send_sem=y_send.at[stage, side], recv_sem=y_recv.at[stage, side],
            device_id=peer, device_id_type=MESH,
        )

    def x_copy(stage, side):
        out, into = (xlo_out, xhi_in) if side == 0 else (xhi_out, xlo_in)
        peer = tile(wrap(me + (TILES - 1 if side == 0 else 1), TILES))
        return pltpu.make_async_remote_copy(
            src_ref=out.at[stage], dst_ref=into.at[stage],
            send_sem=x_send.at[stage, side], recv_sem=x_recv.at[stage, side],
            device_id=peer, device_id_type=MESH,
        )

    def wide(ref, x, n):
        return jnp.concatenate([ref[:, x + i].reshape(128, 128) for i in range(n)], axis=1)

    def pack_faces(stage, x, rows, n):
        faces = mm(face, rows.astype(BF16)).astype(BF16)
        for i in range(n):
            part = faces[:, i * 128 : (i + 1) * 128]
            ylo_out[stage, x + i] = part[0:32]
            yhi_out[stage, x + i] = part[32:64]

    def make_x(stage, e):
        xlo_out[stage] = e[:, 4:8].astype(BF16)
        xhi_out[stage] = e[:, TX : TX + 4].astype(BF16)

    def send_x(stage):
        for side in range(2):
            x_copy(stage, side).start()

    def receive_x(stage, e):
        for side in range(2):
            x_copy(stage, side).wait_recv()
        e[:, 0:4] = xlo_in[stage].astype(F32)
        e[:, TX + 4 : TX + 8] = xhi_in[stage].astype(F32)

    def along_xz(e, out, at, k, x, n):
        here = e[k, pl.ds(x + 4, n)]
        hi, lo = split(here.reshape(n * TY, NZ))
        res = mm(jnp.concatenate([hi, lo], axis=1), cz[k])
        total = here + (res[:, 0:128] + res[:, 128:]).reshape(n, TY, NZ)
        v, s1 = viscosity[k], speeds[0, k]
        for m in range(1, 5):
            b, a = time_step * curve_weights[m - 1] * v, time_step * slope_weights[m - 1] * s1
            total = total + (b - a) * e[k, pl.ds(x + 4 + m, n)] + (b + a) * e[k, pl.ds(x + 4 - m, n)]
        out[k, pl.ds(x + at, n)] = total

    def along_y(e, out, at, x):
        hi, lo = split(wide(e, x + 4, 8))
        res = mm(wy[...], jnp.concatenate([hi, lo], axis=0))
        res = res[0:128] + res[128:]
        for n in range(8):
            out[:, x + at + n] = out[:, x + at + n] + res[:, n * 128 : (n + 1) * 128].reshape(V, TY, NZ)

    def from_halo(stage, x, n):
        rhs = jnp.concatenate(
            [jnp.concatenate([ylo_in[stage, x + i], yhi_in[stage, x + i]], axis=0) for i in range(n)], axis=1
        )
        res = mm(wh[...], rhs)
        return res[0:128] + res[128:]

    load.wait()
    make_x(0, e1)

    @pl.loop(0, TX // 8)
    def _(i):
        pack_faces(0, i * 8, wide(e1, i * 8 + 4, 8), 8)

    square = (128, 128)
    turn = (iota(square, 0) - iota(square, 1)) & 127
    turn = jnp.where(turn > 64, turn - 128, turn)
    z_curve, z_slope = curve_of(turn), slope_of(turn)
    y_shape = (TY, 128)
    y_dist = (iota(y_shape, 1) & 15) - iota(y_shape, 0)
    y_var = lax.shift_right_logical(iota(y_shape, 1), 4)
    y_curve = jnp.where(y_dist == 0, time_step * 3.0 * curve_center, curve_of(y_dist))
    y_slope = slope_of(y_dist)
    h_shape = (TY, 64)
    h_col = iota(h_shape, 1)
    h_dist = (h_col & 3) - 4 + lax.shift_right_logical(h_col, 5) * 20 - iota(h_shape, 0)
    h_var = lax.shift_right_logical(h_col, 2) & 7
    h_curve, h_slope = curve_of(h_dist), slope_of(h_dist)

    @pl.loop(0, V)
    def _(k):
        v, s2, s3 = viscosity[k], speeds[1, k], speeds[2, k]
        ch, cl = split(v * z_curve + s3 * z_slope)
        cz[k] = jnp.concatenate(
            [jnp.concatenate([ch, cl], axis=1), jnp.concatenate([ch, jnp.zeros_like(cl)], axis=1)], axis=0
        )
        w = jnp.where(y_var == k, v * y_curve + s2 * y_slope, 0.0)
        for j in range(V):
            w = w + jnp.where((y_var == j) & (y_dist == 0), time_step * reaction[k, j], 0.0)
        hi, lo = split(w)
        at = pl.ds(pl.multiple_of(k * TY, TY), TY)
        at2 = pl.ds(pl.multiple_of(128 + k * TY, TY), TY)
        wy[at, :] = jnp.concatenate([hi, hi], axis=1)
        wy[at2, :] = jnp.concatenate([lo, jnp.zeros_like(lo)], axis=1)
        hi, lo = split(jnp.where(h_var == k, v * h_curve + s2 * h_slope, 0.0))
        wh[at, :] = hi
        wh[at2, :] = lo

    pl.semaphore_wait(barrier, TILES - 1 + ROWS - 1)
    send_x(0)
    for side in range(2):
        y_copy(0, side).start()

    for p in range(TILES):
        count = jnp.int32(0)
        place = [jnp.int32(0)] * MOST
        valid = [jnp.int32(0)] * MOST
        for u in range(UNITS):
            hit = table[gy, 0, u] == p
            for m in range(MOST):
                take = hit & (count == m)
                place[m] = jnp.where(take, UNIT_ORDER.index(u), place[m])
                valid[m] = jnp.where(take, 1, valid[m])
            count = count + hit.astype(jnp.int32)
        for m in range(MOST):
            picks[p, m] = place[m]
            picks[p, MOST + m] = valid[m]

    hi, lo = split(start_ref[...])
    start_t[...] = jnp.zeros((2 * RP, NX), BF16)
    start_t[0:R, :] = hi
    start_t[RP : RP + R, :] = lo

    @pl.loop(0, V, unroll=2)
    def _(k):
        along_xz(e1, e2, 4, k, 8, 16)
        along_xz(e1, e2, 4, k, 24, 16)

    @pl.loop(1, TX // 8 - 1)
    def _(i):
        along_y(e1, e2, 4, i * 8)

    receive_x(0, e1)

    @pl.loop(0, V, unroll=2)
    def _(k):
        along_xz(e1, e2, 4, k, 0, 8)
        along_xz(e1, e2, 4, k, TX - 8, 8)

    for x in (0, TX - 8):
        along_y(e1, e2, 4, x)

    for side in range(2):
        y_copy(0, side).wait_recv()

    @pl.loop(0, TX // 8)
    def _(i):
        x = i * 8
        rows = wide(e2, x + 4, 8) + from_halo(0, x, 8)
        for j in range(8):
            e2[:, x + 4 + j] = rows[:, j * 128 : (j + 1) * 128].reshape(V, TY, NZ)
        pack_faces(1, x, rows, 8)

    make_x(1, e2)
    send_x(1)
    for side in range(2):
        y_copy(1, side).start()

    def order_lines(part, c):
        pick = pick_early if part == 0 else pick_late
        at = slice(c * CH, c * CH + CH)

        @pl.loop(0, V // 2, unroll=2)
        def _(i):
            both_k = []
            for k in (i * 2, i * 2 + 1):
                lines = acc[k, at]
                if part == 0:
                    lines = 0.5 * (e1[k, c * CH + 4 : c * CH + CH + 4] + lines)
                    acc[k, at] = lines
                both_k.append(lines.reshape(CH * TY, NZ).astype(BF16))
            got = mm(pick, jnp.concatenate(both_k, axis=1)).astype(BF16)
            for n in range(2):
                for j in range(2):
                    for u in range(4):
                        r = (j * 4 + u) * 16
                        lane = part * 512 + u * 128
                        sbuf[i * 2 + n, j, at, lane : lane + 128] = got[r : r + 16, n * 128 : n * 128 + 128]

    def s_copy(part, n, arrival):
        g, x, peer = tile_at(n, back=arrival)
        source = peer if arrival else me
        lanes = pl.ds(part * 512, 512)
        return pltpu.make_async_remote_copy(
            src_ref=sbuf.at[lax.div(peer, 2), lax.rem(peer, 2), :, lanes],
            dst_ref=srec.at[pl.ds(pl.multiple_of(source * TX, TX), TX), lanes],
            send_sem=s_send.at[part, n], recv_sem=s_recv.at[part, n],
            device_id=(g, x, gy), device_id_type=MESH,
        )

    mine = pl.ds(pl.multiple_of(me * TX, TX), TX)

    def send_lines(part):
        for n in range(15):
            s_copy(part, n, False).start()
        lanes = slice(part * 512, part * 512 + 512)
        srec[mine, lanes] = sbuf[lax.div(me, 2), lax.rem(me, 2), :, lanes]

    def receive_lines(part):
        for n in range(15):
            s_copy(part, n, True).wait_recv()

    def add_product(part):
        lanes = slice(part * 512, part * 512 + 512)
        res = mm(start_t[...], srec[:, lanes])
        hi, lo = split(res[0:RP] + res[RP:])
        right = jnp.concatenate([hi, lo], axis=0)

        @pl.loop(0, NX // 256)
        def _(i):
            at = pl.ds(pl.multiple_of(i * 256, 256), 256)
            got = mm_nt(srec[at, lanes], right)
            got = got[:, 0:RP] + got[:, RP:]
            if part == 0:
                pacc[at, :] = got
            else:
                got = pacc[at, :] + got
                pacc[at, :] = got
                psend[at, :] = got.astype(BF16)

    for n, c in enumerate(CHUNK_ORDER):
        if n == 1:
            receive_x(1, e2)

        @pl.loop(0, V, unroll=4)
        def _(k):
            along_xz(e2, acc, 0, k, c * CH, CH)

        for i in range(CH // 8):
            along_y(e2, acc, 0, c * CH + i * 8)
        order_lines(0, c)

    for side in range(2):
        y_copy(1, side).wait_recv()
    send_lines(0)
    for c in range(CHUNKS):
        for i in range(CH // 8):
            x = c * CH + i * 8
            rows = 0.5 * from_halo(1, x, 8)
            for j in range(8):
                acc[:, x + j] = acc[:, x + j] + rows[:, j * 128 : (j + 1) * 128].reshape(V, TY, NZ)
        order_lines(1, c)

    send_lines(1)
    receive_lines(0)
    add_product(0)
    receive_lines(1)
    add_product(1)

    def p_copy(n, arrival):
        g, x, peer = tile_at(n, back=arrival)
        to, source = (me, peer) if arrival else (peer, me)
        return pltpu.make_async_remote_copy(
            src_ref=psend.at[pl.ds(pl.multiple_of(to * TX, TX), TX)], dst_ref=prec.at[source],
            send_sem=p_send.at[n], recv_sem=p_recv.at[n], device_id=(g, x, gy), device_id_type=MESH,
        )

    for n in range(15):
        p_copy(n, False).start()
    prec[me] = psend[mine, :]
    for n in range(15):
        p_copy(n, True).wait_recv()

    total = prec[0].astype(F32)
    for i in range(1, TILES):
        total = total + prec[i].astype(F32)
    qrec[gy] = total

    def q_copy(d, peer, source):
        return pltpu.make_async_remote_copy(
            src_ref=qrec.at[gy], dst_ref=qrec.at[source],
            send_sem=q_send.at[d], recv_sem=q_recv.at[d], device_id=row(peer), device_id_type=MESH,
        )

    @pl.loop(1, ROWS)
    def _(d):
        q_copy(d, wrap(gy + d, ROWS), gy).start()

    @pl.loop(1, ROWS)
    def _(d):
        q_copy(d, gy, wrap(gy + ROWS - d, ROWS)).wait_recv()

    total = qrec[0]
    for i in range(1, ROWS):
        total = total + qrec[i]
    pfull[mine, :] = total

    def rows_of(i):
        return pl.ds(pl.multiple_of(i * TX, TX), TX)

    def f_copy(n, arrival):
        g, x, peer = tile_at(n, back=arrival)
        at = rows_of(peer if arrival else me)
        return pltpu.make_async_remote_copy(
            src_ref=pfull.at[at], dst_ref=pfull.at[at],
            send_sem=f_send.at[n], recv_sem=f_recv.at[n], device_id=(g, x, gy), device_id_type=MESH,
        )

    def f_pass(n, arrival):
        g, x, peer = tile_at(n, back=True)
        _, x2, partner = tile_at(PARTNER)
        at = rows_of(peer - lax.rem(gx, 2) + lax.rem(x2, 2) if arrival else peer)
        return pltpu.make_async_remote_copy(
            src_ref=pfull.at[at], dst_ref=pfull.at[at],
            send_sem=g_send.at[n], recv_sem=g_recv.at[n], device_id=(grp, x2, gy), device_id_type=MESH,
        )

    for n in SAME_CORE + (PARTNER,):
        f_copy(n, False).start()
    for n in SAME_CORE:
        f_copy(n, True).wait_recv()
        f_pass(n, False).start()
    f_copy(PARTNER, True).wait_recv()
    for n in SAME_CORE:
        f_pass(n, True).wait_recv()

    product = pfull[...]
    turned = product.T
    prod_t[...] = turned
    norm = jnp.sum(jnp.sum(product * product, axis=0, keepdims=True), axis=1, keepdims=True)
    hi, lo = split(turned)
    inner = mm_nt(hi, hi) + (mm_nt(hi, lo) + mm_nt(lo, hi))
    inner = inner / norm
    ident = (iota(square, 0) == iota(square, 1)).astype(F32)
    chain = None
    for n in range(NEWTON):
        factor = 1.5 * ident - 0.5 * inner
        chain = factor if n == 0 else both(factor, chain)
        if n < NEWTON - 1:
            inner = both(factor, both(inner, factor))
    basis_t = both(chain, prod_t[...]) / jnp.sqrt(norm)
    half = basis_t.astype(BF16)
    for u in range(UNITS):
        got = mm(half, srec[:, u * 128 : (u + 1) * 128])
        blocks[u] = got[0:R].astype(BF16)

    @pl.loop(0, TILES)
    def _(p):
        for m in range(MOST):
            got = blocks[picks[p, m]]
            csend[p, m] = jnp.where(picks[p, MOST + m] == 1, got, jnp.zeros_like(got))

    def c_copy(n, arrival):
        g, x, peer = tile_at(n, back=arrival)
        to, source = (me, peer) if arrival else (peer, me)
        return pltpu.make_async_remote_copy(
            src_ref=csend.at[to], dst_ref=crec.at[source],
            send_sem=c_send.at[n], recv_sem=c_recv.at[n], device_id=(g, x, gy), device_id_type=MESH,
        )

    for n in range(15):
        c_copy(n, False).start()
    crec[me] = csend[me]
    for n in range(15):
        c_copy(n, True).wait_recv()

    for stage in range(2):
        for side in range(2):
            x_copy(stage, side).wait_send()
            y_copy(stage, side).wait_send()

    for n in range(15):
        for part in range(2):
            s_copy(part, n, False).wait_send()
        p_copy(n, False).wait_send()
        c_copy(n, False).wait_send()
    for n in SAME_CORE:
        f_copy(n, False).wait_send()
        f_pass(n, False).wait_send()
    f_copy(PARTNER, False).wait_send()

    @pl.loop(1, ROWS)
    def _(d):
        q_copy(d, wrap(gy + d, ROWS), gy).wait_send()


def unpack(final_ref, core_ref, final_out, out_hbm, out, final_sem, store_sem):
    final = pltpu.make_async_copy(final_ref, final_out, final_sem)
    final.start()
    stores = [pltpu.make_async_copy(out.at[m], out_hbm.at[m], store_sem.at[m]) for m in range(MOST)]
    for m in range(MOST):
        for s in range(TILES):
            out[m, :, s, :] = core_ref[s, m].astype(F32)
        stores[m].start()
    final.wait()
    for store in stores:
        store.wait()


def on_device(flow_state, speeds, viscosity, reaction, start_basis, slab_table):
    dma = pltpu.SemaphoreType.DMA
    vmem = pltpu.VMEM
    halo_y = vmem((2, TX, 32, NZ), BF16)
    halo_x = vmem((2, V, 4, TY, NZ), BF16)
    hbm = pl.BlockSpec(memory_space=pl.ANY)
    smem = pl.BlockSpec(memory_space=pltpu.SMEM)
    vm = pl.BlockSpec(memory_space=pltpu.VMEM)
    final_state, cores = pl.pallas_call(
        kernel,
        name="sections_and_core",
        out_shape=(vmem((V, TX, TY, NZ), F32), vmem((TILES, MOST, R, NZ), BF16)),
        in_specs=[hbm, smem, smem, smem, vm, smem],
        out_specs=(vm, vm),
        scratch_shapes=[
            vmem((V, TX + 8, TY, NZ), F32),
            vmem((V, TX + 8, TY, NZ), F32),
            halo_y, halo_y, halo_y, halo_y,
            halo_x, halo_x, halo_x, halo_x,
            vmem((V, 2, TX, UNITS * NZ), BF16),
            vmem((NX, UNITS * NZ), BF16),
            vmem((V, 256, 256), BF16),
            vmem((256, 256), BF16),
            vmem((256, 64), BF16),
            vmem((2 * RP, NX), BF16),
            vmem((NX, RP), F32),
            vmem((NX, RP), BF16),
            vmem((TILES, TX, RP), BF16),
            vmem((ROWS, TX, RP), F32),
            vmem((NX, RP), F32),
            vmem((RP, NX), F32),
            vmem((UNITS, R, NZ), BF16),
            vmem((TILES, MOST, R, NZ), BF16),
            pltpu.SMEM((TILES, 2 * MOST), jnp.int32),
            dma(()),
            dma((2, 2)), dma((2, 2)), dma((2, 2)), dma((2, 2)),
            dma((2, 15)), dma((2, 15)),
            dma((15,)), dma((15,)), dma((ROWS,)), dma((ROWS,)),
            dma((15,)), dma((15,)), dma((15,)), dma((15,)), dma((15,)), dma((15,)),
        ],
        compiler_params=pltpu.CompilerParams(
            collective_id=0, has_side_effects=True, vmem_limit_bytes=60 * 1024 * 1024
        ),
    )(flow_state, speeds, viscosity, reaction, start_basis.T, slab_table.transpose(0, 2, 1))
    final_state, core_slots = pl.pallas_call(
        unpack,
        name="unpack_core",
        out_shape=(
            jax.ShapeDtypeStruct((V, TX, TY, NZ), F32),
            jax.ShapeDtypeStruct((MOST, R, TILES, NZ), F32),
        ),
        in_specs=[vm, vm],
        out_specs=(hbm, hbm),
        scratch_shapes=[
            vmem((MOST, R, TILES, NZ), F32),
            dma(()), dma((MOST,)),
        ],
        compiler_params=pltpu.CompilerParams(vmem_limit_bytes=32 * 1024 * 1024),
    )(final_state, cores)
    return final_state, core_slots.reshape(MOST, R, V, 2, NZ)


def solution(mesh):
    field = P(None, ("grp", "gx"), "gy", None)
    return jax.shard_map(
        on_device,
        mesh=mesh,
        in_specs=(field, P(), P(), P(), P(), P()),
        out_specs=(field, P(("grp", "gx", "gy"), None, None, None, None)),
        check_vma=False,
    )
```

time: 116 us -> 92.3 us (0.80)
  Pallas kernels: 106 us -> 91 us
  local copies, waits for them, and re-layouts: 8.17 us -> 0 us
    pallas_call x2, Pallas kernels: 106 us -> 91 us  [the longest x1 88.8 us: on_device(): pl.pallas_call(kernel, name='sections_and_core', out_shape=(vmem((V, TX,...]
    unnamed x5 -> x0, local copies, waits for them, and re-layouts: 8.17 us -> none
where the time goes in v2:
time: 92.3 us; the launch traced here: 91.7 us
  Pallas kernels  91 us (99%)
    pallas_call x1, Pallas kernels, on_device(): pl.pallas_call(kernel, name='sections_and_core', out_shape=(vmem((V, TX,...  88.8 us
    pallas_call x1, Pallas kernels, on_device(): pl.pallas_call(unpack, name='unpack_core', out_shape=(jax.ShapeDtypeStruc...  2.2 us

profile of v2, /device:TPU:1, one launch (start us, length us, event | category | flops | bytes accessed | tf_op | source)
XLA Modules:
  0.0 91.7 jit_solution(12715213587726110786)
XLA Ops:
  0.6 88.8 %sections_and_core.1 = (f32[8,48,16,128]{3,2,1,0:T(8,128)S(1)}, bf16[16,2,96,128]{3,2,1,0:T(8,128)(2,1)S(1)}) custom-call(f32[8,48,16,128]{3,2,1,0:T(8,128)} %flow_hbm.1, f32[3,8]{1,0:T(4,128)} %speeds.1, f32[8]{0:T(128)} %viscosity.1, f32[8,8]{1,0:T(8,128)} %reaction.1, f32[96,768]{1,0:T(8,128)} %bitcast.5, s32[8,1,8]{2,1,0:T(1,128)} %bitcast.6), custom_call_target="tpu_custom_call" | custom-call | tf_op jit(solution)/shard_map/sections_and_core/pallas_call | solution.py:549
  89.5 2.2 %unpack_core.1 = (f32[8,48,16,128]{3,2,1,0:T(8,128)}, f32[2,96,16,128]{3,2,1,0:T(8,128)}) custom-call(f32[8,48,16,128]{3,2,1,0:T(8,128)S(1)} %get-tuple-element.6.final_ref, bf16[16,2,96,128]{3,2,1,0:T(8,128)(2,1)S(1)} %get-tuple-element.7.core_ref), custom_call_target="tpu_custom_call" | custom-call | tf_op jit(solution)/shard_map/unpack_core/pallas_call | solution.py:585

commit v3 on v2

--- a/solution.py
+++ b/solution.py
@@ -19,7 +19,6 @@
 NEWTON = 5
 CH = 16
 CHUNKS = TX // CH
-CHUNK_ORDER = (1, 0, 2)
 PEERS = (
     (2, 1, 0), (1, 0, 0), (3, 0, 0), (0, 1, 0), (2, 1, 1), (1, 0, 1), (3, 0, 1), (0, 1, 1),
     (2, 0, 0), (1, 1, 0), (3, 1, 0), (2, 0, 1), (1, 1, 1), (3, 1, 1), (0, 0, 1),
@@ -294,16 +293,21 @@
     for side in range(2):
         y_copy(0, side).wait_recv()
 
-    @pl.loop(0, TX // 8)
-    def _(i):
-        x = i * 8
+    def finish_first(x):
         rows = wide(e2, x + 4, 8) + from_halo(0, x, 8)
         for j in range(8):
             e2[:, x + 4 + j] = rows[:, j * 128 : (j + 1) * 128].reshape(V, TY, NZ)
         pack_faces(1, x, rows, 8)
 
+    for x in (0, TX - 8):
+        finish_first(x)
     make_x(1, e2)
     send_x(1)
+
+    @pl.loop(1, TX // 8 - 1)
+    def _(i):
+        finish_first(i * 8)
+
     for side in range(2):
         y_copy(1, side).start()
 
@@ -357,7 +361,7 @@
         hi, lo = split(res[0:RP] + res[RP:])
         right = jnp.concatenate([hi, lo], axis=0)
 
-        @pl.loop(0, NX // 256)
+        @pl.loop(0, NX // 256, unroll=3)
         def _(i):
             at = pl.ds(pl.multiple_of(i * 256, 256), 256)
             got = mm_nt(srec[at, lanes], right)
@@ -369,18 +373,27 @@
                 pacc[at, :] = got
                 psend[at, :] = got.astype(BF16)
 
-    for n, c in enumerate(CHUNK_ORDER):
-        if n == 1:
-            receive_x(1, e2)
-
-        @pl.loop(0, V, unroll=4)
-        def _(k):
-            along_xz(e2, acc, 0, k, c * CH, CH)
-
-        for i in range(CH // 8):
-            along_y(e2, acc, 0, c * CH + i * 8)
+    @pl.loop(0, V, unroll=2)
+    def _(k):
+        along_xz(e2, acc, 0, k, 8, 16)
+        along_xz(e2, acc, 0, k, 24, 16)
+
+    @pl.loop(1, TX // 8 - 1)
+    def _(i):
+        along_y(e2, acc, 0, i * 8)
+
+    order_lines(0, 1)
+    receive_x(1, e2)
+
+    @pl.loop(0, V, unroll=2)
+    def _(k):
+        along_xz(e2, acc, 0, k, 0, 8)
+        along_xz(e2, acc, 0, k, TX - 8, 8)
+
+    for x in (0, TX - 8):
+        along_y(e2, acc, 0, x)
+    for c in (0, 2):
         order_lines(0, c)
-
     for side in range(2):
         y_copy(1, side).wait_recv()
     send_lines(0)
@@ -458,7 +471,7 @@
 
     for n in SAME_CORE + (PARTNER,):
         f_copy(n, False).start()
-    for n in SAME_CORE:
+    for n in SAME_CORE[1:] + SAME_CORE[:1]:
         f_copy(n, True).wait_recv()
         f_pass(n, False).start()
     f_copy(PARTNER, True).wait_recv()
@@ -481,9 +494,10 @@
             inner = both(factor, both(inner, factor))
     basis_t = both(chain, prod_t[...]) / jnp.sqrt(norm)
     half = basis_t.astype(BF16)
-    for u in range(UNITS):
-        got = mm(half, srec[:, u * 128 : (u + 1) * 128])
-        blocks[u] = got[0:R].astype(BF16)
+    for u in range(0, UNITS, 4):
+        got = mm(half, srec[:, u * 128 : (u + 4) * 128])[0:R].astype(BF16)
+        for i in range(4):
+            blocks[u + i] = got[:, i * 128 : (i + 1) * 128]
 
     @pl.loop(0, TILES)
     def _(p):

time: 92.3 us -> 91.7 us (level)
  no operation moved by 1% of the time
where the time goes in v3:
time: 91.7 us; the launch traced here: 91.6 us
  Pallas kernels  90.9 us (99%)
    pallas_call x1, Pallas kernels, on_device(): pl.pallas_call(kernel, name='sections_and_core', out_shape=(vmem((V, TX,...  88.7 us
    pallas_call x1, Pallas kernels, on_device(): pl.pallas_call(unpack, name='unpack_core', out_shape=(jax.ShapeDtypeStruc...  2.2 us

profile of v3, /device:TPU:1, one launch (start us, length us, event | category | flops | bytes accessed | tf_op | source)
XLA Modules:
  0.0 91.6 jit_solution(15506712214241409683)
XLA Ops:
  0.6 88.7 %sections_and_core.1 = (f32[8,48,16,128]{3,2,1,0:T(8,128)S(1)}, bf16[16,2,96,128]{3,2,1,0:T(8,128)(2,1)S(1)}) custom-call(f32[8,48,16,128]{3,2,1,0:T(8,128)} %flow_hbm.1, f32[3,8]{1,0:T(4,128)} %speeds.1, f32[8]{0:T(128)} %viscosity.1, f32[8,8]{1,0:T(8,128)} %reaction.1, f32[96,768]{1,0:T(8,128)} %bitcast.5, s32[8,1,8]{2,1,0:T(1,128)} %bitcast.6), custom_call_target="tpu_custom_call" | custom-call | tf_op jit(solution)/shard_map/sections_and_core/pallas_call | solution.py:563
  89.4 2.2 %unpack_core.1 = (f32[8,48,16,128]{3,2,1,0:T(8,128)}, f32[2,96,16,128]{3,2,1,0:T(8,128)}) custom-call(f32[8,48,16,128]{3,2,1,0:T(8,128)S(1)} %get-tuple-element.6.final_ref, bf16[16,2,96,128]{3,2,1,0:T(8,128)(2,1)S(1)} %get-tuple-element.7.core_ref), custom_call_target="tpu_custom_call" | custom-call | tf_op jit(solution)/shard_map/unpack_core/pallas_call | solution.py:599

commit v4 on v3

--- a/solution.py
+++ b/solution.py
@@ -499,11 +499,10 @@
         for i in range(4):
             blocks[u + i] = got[:, i * 128 : (i + 1) * 128]
 
-    @pl.loop(0, TILES)
-    def _(p):
+    def pick_blocks(p, out, at):
         for m in range(MOST):
             got = blocks[picks[p, m]]
-            csend[p, m] = jnp.where(picks[p, MOST + m] == 1, got, jnp.zeros_like(got))
+            out[at, m] = jnp.where(picks[p, MOST + m] == 1, got, jnp.zeros_like(got))
 
     def c_copy(n, arrival):
         g, x, peer = tile_at(n, back=arrival)
@@ -514,8 +513,10 @@
         )
 
     for n in range(15):
+        peer = tile_at(n)[2]
+        pick_blocks(peer, csend, peer)
         c_copy(n, False).start()
-    crec[me] = csend[me]
+    pick_blocks(me, crec, me)
     for n in range(15):
         c_copy(n, True).wait_recv()
 

time: 91.7 us -> 91.4 us (level)
  no operation moved by 1% of the time
where the time goes in v4:
time: 91.4 us; the launch traced here: 91.3 us
  Pallas kernels  90.6 us (99%)
    pallas_call x1, Pallas kernels, on_device(): pl.pallas_call(kernel, name='sections_and_core', out_shape=(vmem((V, TX,...  88.4 us
    pallas_call x1, Pallas kernels, on_device(): pl.pallas_call(unpack, name='unpack_core', out_shape=(jax.ShapeDtypeStruc...  2.2 us

profile of v4, /device:TPU:1, one launch (start us, length us, event | category | flops | bytes accessed | tf_op | source)
XLA Modules:
  0.0 91.3 jit_solution(6921315813639199256)
XLA Ops:
  0.6 88.4 %sections_and_core.1 = (f32[8,48,16,128]{3,2,1,0:T(8,128)S(1)}, bf16[16,2,96,128]{3,2,1,0:T(8,128)(2,1)S(1)}) custom-call(f32[8,48,16,128]{3,2,1,0:T(8,128)} %flow_hbm.1, f32[3,8]{1,0:T(4,128)} %speeds.1, f32[8]{0:T(128)} %viscosity.1, f32[8,8]{1,0:T(8,128)} %reaction.1, f32[96,768]{1,0:T(8,128)} %bitcast.5, s32[8,1,8]{2,1,0:T(1,128)} %bitcast.6), custom_call_target="tpu_custom_call" | custom-call | tf_op jit(solution)/shard_map/sections_and_core/pallas_call | solution.py:564
  89.1 2.2 %unpack_core.1 = (f32[8,48,16,128]{3,2,1,0:T(8,128)}, f32[2,96,16,128]{3,2,1,0:T(8,128)}) custom-call(f32[8,48,16,128]{3,2,1,0:T(8,128)S(1)} %get-tuple-element.6.final_ref, bf16[16,2,96,128]{3,2,1,0:T(8,128)(2,1)S(1)} %get-tuple-element.7.core_ref), custom_call_target="tpu_custom_call" | custom-call | tf_op jit(solution)/shard_map/unpack_core/pallas_call | solution.py:600
